TPU v7x, 32 devices: a whole 2x2x4 slice. The times are simulated.
32 devices in a mesh: grp: 4 (over y, core), dev: 8 (over z, x).
Axes of the slice: x: 2, y: 2, z: 4, core: 2. Of those that a mesh axis runs over, the one named last changes fastest.
Arguments:
- colloc: bfloat16 [3072, 8000], P('dev', 'grp'), may hold values from -3 to 3
- block_colloc: bfloat16 [1024, 8000], P('dev', 'grp'), may hold values from -3 to 3
- factor: float32 [3072, 8192], P('dev', 'grp'), may hold values from -4.8 to 4.8
- block_factor: float32 [1024, 8192], P('dev', 'grp'), may hold values from -0.25 to 0.25
Outputs:
- block_lower: float32 [1024, 1024], P('dev')
- panel_lower: float32 [8, 384, 1024], P('dev', 'grp')
All inputs are finite; a program needn't handle non-finite values.
Results may differ from a plain program's by a relative error of at most 0.0003.
Values may be sent and summed in bfloat16 or wider, within the bound.
No kernel may reach another device: no remote copies, remote signals or barrier semaphores. Data moves between devices by JAX's collectives and lax.ppermute only.
A program may use at most 64 MiB of HBM per device.

v0:
```python
import jax
import jax.numpy as jnp
from jax import lax
from jax.sharding import PartitionSpec as P

DAMPING = 0.0625


def with_damping(gram_part, update_part, row_index, col_index):
    return (
        gram_part * gram_part
        + jnp.where(row_index == col_index, jnp.float32(DAMPING), jnp.float32(0.0))
        - update_part
    )


def on_device(colloc, block_colloc, factor, block_factor):
    grp_count = lax.axis_size("grp")
    grp_index = lax.axis_index("grp")
    dev_index = lax.axis_index("dev")
    band_rows = block_colloc.shape[0]
    panel_width = band_rows * lax.axis_size("dev")
    points = jnp.concatenate([block_colloc, colloc], axis=0)
    earlier = jnp.concatenate([block_factor, factor], axis=0)
    metric_terms = lax.dot_general(
        points,
        lax.all_gather(block_colloc, "dev", axis=0, tiled=True),
        (((1,), (1,)), ((), ())),
        preferred_element_type=jnp.float32,
    )
    update_terms = lax.dot_general(
        earlier,
        lax.all_gather(block_factor, "dev", axis=0, tiled=True),
        (((1,), (1,)), ((), ())),
        precision=lax.Precision.HIGHEST,
        preferred_element_type=jnp.float32,
    )
    gram_low, update_low = (
        lax.psum_scatter(metric_terms[band_rows:], "grp", scatter_dimension=0, tiled=True),
        lax.psum_scatter(update_terms[band_rows:], "grp", scatter_dimension=0, tiled=True),
    )
    below_rows = gram_low * gram_low - update_low
    gram_head = metric_terms[:band_rows]
    update_head = update_terms[:band_rows]
    row_index = dev_index * band_rows + lax.broadcasted_iota(jnp.int32, (band_rows, 1), 0)
    slice_width = panel_width // grp_count
    slice_index = grp_index * slice_width + lax.broadcasted_iota(jnp.int32, (1, slice_width), 1)
    gram_slice, update_slice = (
        lax.psum_scatter(gram_head, "grp", scatter_dimension=1, tiled=True),
        lax.psum_scatter(update_head, "grp", scatter_dimension=1, tiled=True),
    )
    own_slice = with_damping(gram_slice, update_slice, row_index, slice_index)
    row_slab = lax.all_gather(own_slice, "grp", axis=1, tiled=True)
    schur = lax.all_gather(row_slab, "dev", axis=0, tiled=True)
    cholesky_factor = jnp.linalg.cholesky(schur)
    panel_rows = lax.linalg.triangular_solve(
        cholesky_factor, below_rows, left_side=False, lower=True, transpose_a=True
    )
    factor_rows = lax.dynamic_slice_in_dim(cholesky_factor, dev_index * band_rows, band_rows, 0)
    return (factor_rows, panel_rows[None])


def solution(mesh):
    placed = (P("dev", "grp"), P("dev", "grp"), P("dev", "grp"), P("dev", "grp"))
    return jax.shard_map(
        on_device,
        mesh=mesh,
        in_specs=placed,
        out_specs=(P("dev", None), P("dev", "grp", None)),
        check_vma=False,
    )
```

profile of v0, /device:TPU:0, one launch (start us, length us, event | category | flops | bytes accessed | tf_op | source)
XLA Modules:
  0.0 742.4 jit_solution(15804348153405605713)
XLA Ops:
  8.7 78.0 %all-gather.4.cloned.1.call-done = bf16[1024,2000]{0,1:T(8,128)(2,1)} async-done(((bf16[128,2000]{0,1:T(8,128)(2,1)}), bf16[1024,2000]{0,1:T(8,128)(2,1)}) %all-gather.4.cloned.1.call-update) | async-done | bytes 4096016 | tf_op jit(solution)/shard_map/all_gather | solution.py:27
  86.7 5.1 fusion.6
  91.9 1.0 copy.9
  93.0 119.0 %all-gather.6.cloned.1.call-done = f32[1024,2048]{1,0:T(8,128)} async-done(((f32[128,2048]{1,0:T(8,128)}), f32[1024,2048]{1,0:T(8,128)}) %all-gather.6.cloned.1.call-update) | async-done | bytes 8388624 | tf_op jit(solution)/shard_map/all_gather | solution.py:33
  212.0 16.8 %fusion = f32[512,1024]{1,0:T(8,128)S(1)} fusion(f32[1024,2048]{1,0:T(8,128)} %all-gather.6.cloned.1.call-done, f32[384,2048]{1,0:T(8,128)} %param.6, f32[128,2048]{1,0:T(8,128)} %param.7), kind=kOutput, calls=%fused_computation.2 | convolution fusion | flops 12885950464 | bytes 14680064 | tf_op jit(solution)/shard_map/dot_general | solution.py:31
  228.8 1.3 copy-done.1
  231.2 1.3 slice.252
  232.6 2.8 slice.253
  235.5 23.6 %reduce-scatter.7.cloned.1.call-done = f32[128,256]{0,1:T(8,128)} async-done(((f32[128,1024]{0,1:T(8,128)}), f32[128,256]{0,1:T(8,128)}) %reduce-scatter.7.cloned.1.call-update) | async-done | bytes 131088 | tf_op jit(solution)/shard_map/reduce_scatter | solution.py:50
  259.1 1.1 add_subtract_fusion
  260.2 7.2 all_gather.14
  267.4 22.2 %reduce-scatter.9.cloned.1.call-done = f32[96,1024]{1,0:T(8,128)} async-done(((f32[384,1024]{1,0:T(8,128)}), f32[96,1024]{1,0:T(8,128)}) %reduce-scatter.9.cloned.1.call-update) | async-done | bytes 393232 | tf_op jit(solution)/shard_map/reduce_scatter | solution.py:39
  289.7 30.8 %reduce-scatter.11.cloned.1.call-done = f32[96,1024]{1,0:T(8,128)} async-done(((f32[384,1024]{1,0:T(8,128)}), f32[96,1024]{1,0:T(8,128)}) %reduce-scatter.11.cloned.1.call-update) | async-done | bytes 393232 | tf_op jit(solution)/shard_map/reduce_scatter | solution.py:40
  320.4 1.2 multiply_subtract_fusion
  321.6 75.9 %all-gather.8.cloned.1.call-done = f32[1024,1024]{0,1:T(8,128)} async-done(((f32[128,1024]{0,1:T(8,128)}), f32[1024,1024]{0,1:T(8,128)}) %all-gather.8.cloned.1.call-update) | async-done | bytes 4194320 | tf_op jit(solution)/shard_map/all_gather | solution.py:54
  397.5 5.8 copy.8
  403.4 4.4 fusion.4
  407.8 1.9 copy-done
  409.7 11.7 %cholesky.223 = f32[128,128]{1,0:T(8,128)S(1)} custom-call(f32[128,128]{1,0:T(8,128)S(1)} %cholesky.580), custom_call_target="Cholesky" | custom-call | tf_op jit(solution)/shard_map/jit(cholesky)/cholesky | solution.py:55
  421.5 9.8 %custom-call.62 = f32[1,128,128]{1,2,0:T(8,128)S(1)} custom-call(f32[1,128,128]{2,1,0:T(8,128)S(1)} %get-tuple-element.43), custom_call_target="InvertDiagBlocksLowerTriangular" | custom-call | tf_op jit(solution)/shard_map/jit(cholesky)/cholesky | solution.py:55
  431.3 2.5 cholesky.255
  433.8 2.3 constant_dynamic-update-slice_fusion.32
  436.2 1.5 convolution_subtract_fusion
  437.7 11.9 %cholesky.244 = f32[128,128]{1,0:T(8,128)S(1)} custom-call(f32[128,128]{1,0:T(8,128)S(1)} %cholesky.584), custom_call_target="Cholesky" | custom-call | tf_op jit(solution)/shard_map/jit(cholesky)/cholesky | solution.py:55
  450.2 9.8 %custom-call.63 = f32[1,128,128]{1,2,0:T(8,128)S(1)} custom-call(f32[1,128,128]{2,1,0:T(8,128)S(1)} %get-tuple-element.40), custom_call_target="InvertDiagBlocksLowerTriangular" | custom-call | tf_op jit(solution)/shard_map/jit(cholesky)/cholesky | solution.py:55
  460.1 1.2 convolution_dynamic-update-slice_fusion
  461.3 2.1 convolution_subtract_fusion.1
  463.4 11.7 %cholesky.468 = f32[128,128]{1,0:T(8,128)S(1)} custom-call(f32[128,128]{1,0:T(8,128)S(1)} %cholesky.589), custom_call_target="Cholesky" | custom-call | tf_op jit(solution)/shard_map/jit(cholesky)/cholesky | solution.py:55
  476.4 9.8 %custom-call.64 = f32[1,128,128]{1,2,0:T(8,128)S(1)} custom-call(f32[1,128,128]{2,1,0:T(8,128)S(1)} %get-tuple-element.37), custom_call_target="InvertDiagBlocksLowerTriangular" | custom-call | tf_op jit(solution)/shard_map/jit(cholesky)/cholesky | solution.py:55
  486.2 1.2 convolution_dynamic-update-slice_fusion.1
  487.4 2.3 convolution_subtract_fusion.2
  489.8 11.9 %cholesky.487 = f32[128,128]{1,0:T(8,128)S(1)} custom-call(f32[128,128]{1,0:T(8,128)S(1)} %cholesky.594), custom_call_target="Cholesky" | custom-call | tf_op jit(solution)/shard_map/jit(cholesky)/cholesky | solution.py:55
  503.0 9.8 %custom-call.65 = f32[1,128,128]{1,2,0:T(8,128)S(1)} custom-call(f32[1,128,128]{2,1,0:T(8,128)S(1)} %get-tuple-element.34), custom_call_target="InvertDiagBlocksLowerTriangular" | custom-call | tf_op jit(solution)/shard_map/jit(cholesky)/cholesky | solution.py:55
  512.8 1.1 convolution_dynamic-update-slice_fusion.2
  513.9 2.3 convolution_subtract_fusion.3
  516.2 11.7 %cholesky.506 = f32[128,128]{1,0:T(8,128)S(1)} custom-call(f32[128,128]{1,0:T(8,128)S(1)} %cholesky.599), custom_call_target="Cholesky" | custom-call | tf_op jit(solution)/shard_map/jit(cholesky)/cholesky | solution.py:55
  529.3 10.2 %custom-call.66 = f32[1,128,128]{1,2,0:T(8,128)S(1)} custom-call(f32[1,128,128]{2,1,0:T(8,128)S(1)} %get-tuple-element.31), custom_call_target="InvertDiagBlocksLowerTriangular" | custom-call | tf_op jit(solution)/shard_map/jit(cholesky)/cholesky | solution.py:55
  540.5 2.3 convolution_subtract_fusion.4
  542.8 11.7 %cholesky.526 = f32[128,128]{1,0:T(8,128)S(1)} custom-call(f32[128,128]{1,0:T(8,128)S(1)} %cholesky.604), custom_call_target="Cholesky" | custom-call | tf_op jit(solution)/shard_map/jit(cholesky)/cholesky | solution.py:55
  555.8 9.8 %custom-call.67 = f32[1,128,128]{1,2,0:T(8,128)S(1)} custom-call(f32[1,128,128]{2,1,0:T(8,128)S(1)} %get-tuple-element.28), custom_call_target="InvertDiagBlocksLowerTriangular" | custom-call | tf_op jit(solution)/shard_map/jit(cholesky)/cholesky | solution.py:55
  566.5 2.0 convolution_subtract_fusion.5
  568.6 11.9 %cholesky.546 = f32[128,128]{1,0:T(8,128)S(1)} custom-call(f32[128,128]{1,0:T(8,128)S(1)} %cholesky.609), custom_call_target="Cholesky" | custom-call | tf_op jit(solution)/shard_map/jit(cholesky)/cholesky | solution.py:55
  581.7 9.8 %custom-call.68 = f32[1,128,128]{1,2,0:T(8,128)S(1)} custom-call(f32[1,128,128]{2,1,0:T(8,128)S(1)} %get-tuple-element.25), custom_call_target="InvertDiagBlocksLowerTriangular" | custom-call | tf_op jit(solution)/shard_map/jit(cholesky)/cholesky | solution.py:55
  592.4 1.8 convolution_subtract_fusion.6
  594.2 11.7 %cholesky.564 = f32[128,128]{1,0:T(8,128)S(1)} custom-call(f32[128,128]{1,0:T(8,128)S(1)} %convolution_subtract_fusion.6), custom_call_target="Cholesky" | custom-call | tf_op jit(solution)/shard_map/jit(cholesky)/cholesky | solution.py:55
  612.9 6.6 fusion.5
  619.4 23.2 %while.1 = (s32[]{:T(128)}, f32[1024,1024]{1,0:T(8,128)}, s32[8,2]{0,1:T(2,128)S(1)}, f32[8,128,128]{2,1,0:T(8,128)S(1)}, s32[]{:T(128)}) while((s32[]{:T(128)}, f32[1024,1024]{1,0:T(8,128)}, s32[8,2]{0,1:T(2,128)S(1)}, f32[8,128,128]{2,1,0:T(8,128)S(1)}, s32[]{:T(128)}) %tuple.62), condition=%wide.while_cond, body=%wide.while_body.sunk | while | flops 2 | bytes 131189 | solution.py:56
  620.0 2.3 bitcast_dynamic-update-slice_fusion.2
  623.0 2.3 bitcast_dynamic-update-slice_fusion.2
  625.9 2.3 bitcast_dynamic-update-slice_fusion.2
  628.8 2.3 bitcast_dynamic-update-slice_fusion.2
  631.7 2.3 bitcast_dynamic-update-slice_fusion.2
  634.6 2.3 bitcast_dynamic-update-slice_fusion.2
  637.5 2.3 bitcast_dynamic-update-slice_fusion.2
  640.4 2.2 bitcast_dynamic-update-slice_fusion.2
  642.6 78.8 %custom-call.69 = f32[8,128,128]{1,2,0:T(8,128)S(1)} custom-call(f32[8,128,128]{2,1,0:T(8,128)S(1)} %get-tuple-element.9), custom_call_target="InvertDiagBlocksLowerTriangular" | custom-call | tf_op jit(solution)/shard_map/triangular_solve | solution.py:56
  721.7 1.1 convolution_subtract_fusion.10
  723.0 1.2 convolution_subtract_fusion.9
  724.4 1.3 convolution_subtract_fusion.13
  725.9 1.3 convolution_subtract_fusion.12
  727.4 1.5 convolution_subtract_fusion.11
  729.1 1.5 convolution_subtract_fusion.8
  730.8 1.7 convolution_subtract_fusion.7
  732.5 1.9 constant_dynamic-slice_fusion.1
  (76 shorter events, 22.0 us)
Async XLA Ops:
  7.2 79.5 %all-gather.4.cloned.1.call-start = ((), (), s32[]{:S(2)}) async-start(), calls=%async_computation.4 | async-start | bytes 4608000 | tf_op jit(solution)/shard_map/all_gather | solution.py:27
  7.9 204.1 %all-gather.6.cloned.1.call-start = ((), (), s32[]{:S(2)}) async-start(), calls=%async_computation.6 | async-start | bytes 9437184 | tf_op jit(solution)/shard_map/all_gather | solution.py:33
  8.6 226.9 %reduce-scatter.5.cloned.1.call-start = ((), (), s32[]{:S(2)}) async-start(), calls=%async_computation.5 | async-start | bytes 655360 | tf_op jit(solution)/shard_map/reduce_scatter | solution.py:49
  92.9 166.2 %reduce-scatter.7.cloned.1.call-start = ((), (), s32[]{:S(2)}) async-start(), calls=%async_computation.7 | async-start | bytes 655360 | tf_op jit(solution)/shard_map/reduce_scatter | solution.py:50
  228.8 1.4 copy-start.1
  231.2 58.5 %reduce-scatter.9.cloned.1.call-start = ((), (), s32[]{:S(2)}) async-start(), calls=%async_computation.9 | async-start | bytes 1966080 | tf_op jit(solution)/shard_map/reduce_scatter | solution.py:39
  232.5 87.9 %reduce-scatter.11.cloned.1.call-start = ((), (), s32[]{:S(2)}) async-start(), calls=%async_computation.10 | async-start | bytes 1966080 | tf_op jit(solution)/shard_map/reduce_scatter | solution.py:40
  235.4 162.1 %all-gather.8.cloned.1.call-start = ((), (), s32[]{:S(2)}) async-start(), calls=%async_computation.8 | async-start | bytes 4718592 | tf_op jit(solution)/shard_map/all_gather | solution.py:54
  407.8 1.9 copy-start
  734.6 0.7 copy-start.2
Sparse Core Ops, SparseCore 0:
  10.0 76.5 all-gather.3
  88.8 123.1 all-gather.5
  214.4 19.8 reduce-scatter.4
  237.4 21.6 reduce-scatter.6
  261.5 28.1 reduce-scatter.8
  292.2 28.1 reduce-scatter.10
  322.5 75.0 all-gather.7
where the time goes:
time: 751 us; the launch traced here: 742 us
  waiting for transfers between devices  351 us (47%)
  other arithmetic  264 us (35%)
  matrix products  56.2 us (7%)
  local copies, waits for them, and re-layouts  43.5 us (6%)
  between operations  19.7 us (3%)
    another operation x30, other arithmetic, on_device(): cholesky_factor = jnp.linalg.cholesky(schur)  172 us
    all_gather x1, waiting for transfers between devices, on_device(): lax.all_gather(block_factor, 'dev', axis=0, tiled=True)  119 us
    another operation x3, other arithmetic, on_device(): lax.linalg.triangular_solve(cholesky_factor, below_rows, left_side=False,...  85.4 us
    all_gather x1, waiting for transfers between devices, on_device(): lax.all_gather(block_colloc, 'dev', axis=0, tiled=True)  78 us
    all_gather x1, waiting for transfers between devices, on_device(): schur = lax.all_gather(row_slab, 'dev', axis=0, tiled=True)  75.9 us
    reduce_scatter x1, waiting for transfers between devices, on_device(): lax.psum_scatter(update_terms[band_rows:], 'grp', scatter_dimension=0, ti...  30.8 us
    reduce_scatter x1, waiting for transfers between devices, on_device(): lax.psum_scatter(update_head, 'grp', scatter_dimension=1, tiled=True)  23.6 us
    another operation x24, local copies, waits for them, and re-layouts  23 us
  transfers between devices with their start and end apart: 7, of which 6 were waited for; matrix products, arithmetic and copies ran while one was open for 4% of the time, Pallas kernels for 0%

commit v1 on v0

--- a/solution.py
+++ b/solution.py
@@ -2,8 +2,158 @@
 import jax.numpy as jnp
 from jax import lax
 from jax.sharding import PartitionSpec as P
+from jax.experimental import pallas as pl
+from jax.experimental.pallas import tpu as pltpu
 
 DAMPING = 0.0625
+LANES = 128
+SUBS = 8
+
+
+def split(value):
+    high = value.astype(jnp.bfloat16)
+    low = (value - high.astype(jnp.float32)).astype(jnp.bfloat16)
+    return high, low
+
+
+def dot3(left, right, contract):
+    (left_high, left_low), (right_high, right_low) = left, right
+    dims = (contract, ((), ()))
+
+    def one(a, b):
+        return lax.dot_general(a, b, dims, preferred_element_type=jnp.float32)
+
+    return one(left_high, right_high) + (one(left_high, right_low) + one(left_low, right_high))
+
+
+NN = ((1,), (0,))
+NT = ((1,), (1,))
+
+
+def reciprocal(value):
+    guess = pl.reciprocal(value, approx=True)
+    guess = guess * (2.0 - value * guess)
+    return guess * (2.0 - value * guess)
+
+
+def over_lanes(value, column):
+    return jnp.broadcast_to(value[:, column : column + 1], (SUBS, LANES))
+
+
+def over_subs(value, row):
+    return jnp.broadcast_to(value[row : row + 1, :], (SUBS, LANES))
+
+
+def factor_block(block):
+    lane = lax.broadcasted_iota(jnp.int32, (SUBS, LANES), 1)
+    sub = lax.broadcasted_iota(jnp.int32, (SUBS, LANES), 0)
+    strips = LANES // SUBS
+    rows = [block[SUBS * s : SUBS * (s + 1), :] for s in range(strips)]
+    upper, inverse = [], []
+    for s in range(strips):
+        first = SUBS * s
+        pivots = (lane >= first) & (lane < first + SUBS)
+        own = rows[s]
+        unit = jnp.where(lane - first == sub, 1.0, jnp.where(pivots, 0.0, own))
+        columns = [over_lanes(own, first + k) for k in range(SUBS)]
+        kept_own, kept_unit = own, unit
+        diagonal, scale = None, None
+        for k in range(SUBS):
+            here = sub == k
+            pivot = over_subs(columns[k], k)
+            share = reciprocal(pivot)
+            if k == 0:
+                diagonal, scale = pivot, share
+            else:
+                diagonal = jnp.where(here, pivot, diagonal)
+                scale = jnp.where(here, share, scale)
+                kept_own = jnp.where(here, own, kept_own)
+                kept_unit = jnp.where(here, unit, kept_unit)
+            multiplier = jnp.where(here, 0.0, columns[k] * share)
+            for q in range(k + 1, SUBS):
+                columns[q] = columns[q] - multiplier * over_subs(columns[q], k)
+            own = own - multiplier * over_subs(own, k)
+            unit = unit - multiplier * over_subs(unit, k)
+        root = lax.rsqrt(diagonal)
+        upper.append(jnp.where(lane >= first + sub, kept_own * root, 0.0))
+        inverse.append(jnp.where(lane <= first + sub, kept_unit * root, 0.0))
+        solved = unit * scale
+        spread = [over_subs(solved, k) for k in range(SUBS)]
+        for i in range(s + 1, strips):
+            value = jnp.where(pivots, 0.0, rows[i])
+            for k in range(SUBS):
+                value = value - over_lanes(rows[i], first + k) * spread[k]
+            rows[i] = value
+    return jnp.concatenate(upper, axis=0), jnp.concatenate(inverse, axis=0)
+
+
+def panel_kernel(place_ref, schur_ref, below_ref, rows_ref, panel_ref, low_ref, high_part, low_part):
+    size = schur_ref.shape[0]
+    blocks = size // LANES
+    zero = jnp.zeros((LANES, LANES), jnp.float32)
+
+    def part(j, n=1):
+        return slice(j * LANES, (j + n) * LANES)
+
+    def left(j, count):
+        return split(low_ref[part(j), : count * LANES])
+
+    def right(count, cols):
+        return high_part[: count * LANES, cols], low_part[: count * LANES, cols]
+
+    diagonal = schur_ref[part(0), part(0)]
+    for j in range(blocks):
+        rest = slice((j + 1) * LANES, size)
+        upper, inverse = factor_block(diagonal)
+        inverse_parts = split(inverse)
+        low_ref[part(j), part(j)] = upper.T
+        for i in range(j):
+            low_ref[part(i), part(j)] = zero
+        if j + 1 < blocks:
+            ahead = schur_ref[part(j), rest]
+            next_diagonal = schur_ref[part(j + 1), part(j + 1)]
+            if j:
+                ahead = ahead - dot3(left(j, j), right(j, rest), NN)
+                next_diagonal = next_diagonal - dot3(left(j + 1, j), right(j, part(j + 1)), NN)
+            row = dot3(inverse_parts, split(ahead), NN)
+            row_high, row_low = split(row)
+            high_part[part(j), rest] = row_high
+            low_part[part(j), rest] = row_low
+            for i in range(j + 1, blocks):
+                low_ref[part(i), part(j)] = row[:, part(i - j - 1)].T
+            first = split(low_ref[part(j + 1), part(j)])
+            diagonal = next_diagonal - dot3(first, (row_high[:, :LANES], row_low[:, :LANES]), NN)
+        own = below_ref[:, part(j)]
+        if j:
+            own = own - dot3(split(panel_ref[:, : j * LANES]), right(j, part(j)), NN)
+        panel_ref[:, part(j)] = dot3(split(own), inverse_parts, NT)
+    band = rows_ref.shape[0]
+    start = pl.multiple_of(place_ref[0] * band, SUBS)
+    rows_ref[...] = low_ref[pl.ds(start, band), :]
+
+
+def factor_panel(place, schur, below, band):
+    size = schur.shape[0]
+    return pl.pallas_call(
+        panel_kernel,
+        in_specs=[
+            pl.BlockSpec(memory_space=pltpu.SMEM),
+            pl.BlockSpec(memory_space=pltpu.VMEM),
+            pl.BlockSpec(memory_space=pltpu.VMEM),
+        ],
+        out_specs=[pl.BlockSpec(memory_space=pltpu.VMEM), pl.BlockSpec(memory_space=pltpu.VMEM)],
+        out_shape=[
+            jax.ShapeDtypeStruct((band, size), jnp.float32),
+            jax.ShapeDtypeStruct(below.shape, jnp.float32),
+        ],
+        scratch_shapes=[
+            pltpu.VMEM((size, size), jnp.float32),
+            pltpu.VMEM((size, size), jnp.bfloat16),
+            pltpu.VMEM((size, size), jnp.bfloat16),
+        ],
+        compiler_params=pltpu.CompilerParams(vmem_limit_bytes=40 * 1024 * 1024),
+        name="cholesky_panel",
+    )(place, schur, below)
 
 
 def with_damping(gram_part, update_part, row_index, col_index):
@@ -52,11 +202,8 @@
     own_slice = with_damping(gram_slice, update_slice, row_index, slice_index)
     row_slab = lax.all_gather(own_slice, "grp", axis=1, tiled=True)
     schur = lax.all_gather(row_slab, "dev", axis=0, tiled=True)
-    cholesky_factor = jnp.linalg.cholesky(schur)
-    panel_rows = lax.linalg.triangular_solve(
-        cholesky_factor, below_rows, left_side=False, lower=True, transpose_a=True
-    )
-    factor_rows = lax.dynamic_slice_in_dim(cholesky_factor, dev_index * band_rows, band_rows, 0)
+    place = jnp.reshape(dev_index, (1,)).astype(jnp.int32)
+    factor_rows, panel_rows = factor_panel(place, schur, below_rows, band_rows)
     return (factor_rows, panel_rows[None])
 
 

time: 751 us -> 462 us (0.62)
  other arithmetic: 264 us -> 2.22 us
  Pallas kernels: 0 us -> 49.5 us
  matrix products: 56.2 us -> 21.8 us
  local copies, waits for them, and re-layouts: 43.5 us -> 9.26 us
    another operation x33 -> x0, other arithmetic: 258 us -> none  [the longest x30 172 us: on_device(): cholesky_factor = jnp.linalg.cholesky(schur)]
    pallas_call x0 -> x1, Pallas kernels: none -> 49.5 us  [factor_panel(): pl.pallas_call(panel_kernel, in_specs=[pl.BlockSpec(memory_space=pltpu.SM...]
    another operation x29 -> x0, matrix products: 34.2 us -> none  [the longest x14 23 us: on_device(): cholesky_factor = jnp.linalg.cholesky(schur)]
    another operation x33 -> x0, local copies, waits for them, and re-layouts: 25.6 us -> none
  transfers between devices with their start and end apart: 7 -> 7, of which waited for: 6 -> 6; matrix products, arithmetic and copies ran while one was open for 4% -> 7% of each run, Pallas kernels for 0% -> 0%
where the time goes in v1:
time: 462 us; the launch traced here: 455 us
  waiting for transfers between devices  350 us (76%)
  Pallas kernels  49.5 us (11%)
  matrix products  21.8 us (5%)
  between operations  14.6 us (3%)
  local copies, waits for them, and re-layouts  9.26 us (2%)
  blocking collectives  7.41 us (2%)
    all_gather x1, waiting for transfers between devices, on_device(): lax.all_gather(block_factor, 'dev', axis=0, tiled=True)  119 us
    all_gather x1, waiting for transfers between devices, on_device(): lax.all_gather(block_colloc, 'dev', axis=0, tiled=True)  78 us
    all_gather x1, waiting for transfers between devices, on_device(): schur = lax.all_gather(row_slab, 'dev', axis=0, tiled=True)  74.4 us
    pallas_call x1, Pallas kernels, factor_panel(): pl.pallas_call(panel_kernel, in_specs=[pl.BlockSpec(memory_space=pltpu.SM...  49.5 us
    reduce_scatter x1, waiting for transfers between devices, on_device(): lax.psum_scatter(update_terms[band_rows:], 'grp', scatter_dimension=0, ti...  30.8 us
    reduce_scatter x1, waiting for transfers between devices, on_device(): lax.psum_scatter(update_head, 'grp', scatter_dimension=1, tiled=True)  24 us
    reduce_scatter x1, waiting for transfers between devices, on_device(): lax.psum_scatter(metric_terms[band_rows:], 'grp', scatter_dimension=0, ti...  22.1 us
    dot_general x1, matrix products, on_device(): lax.dot_general(earlier, lax.all_gather(block_factor, 'dev', axis=0, tile...  16.6 us
  transfers between devices with their start and end apart: 7, of which 6 were waited for; matrix products, arithmetic and copies ran while one was open for 7% of the time, Pallas kernels for 0%

profile of v1, /device:TPU:0, one launch (start us, length us, event | category | flops | bytes accessed | tf_op | source)
XLA Modules:
  0.0 455.0 jit_solution(15660259515012978492)
XLA Ops:
  7.2 0.0 all-gather.4.cloned.1.call-start
  7.2 0.7 all-gather.4.cloned.1.call-update
  7.9 0.0 all-gather.6.cloned.1.call-start
  7.9 0.7 all-gather.6.cloned.1.call-update
  8.6 0.0 copy-start.2
  8.7 0.0 reduce-scatter.5.cloned.1.call-start
  8.7 78.0 %all-gather.4.cloned.1.call-done = bf16[1024,2000]{0,1:T(8,128)(2,1)} async-done(((bf16[128,2000]{0,1:T(8,128)(2,1)}), bf16[1024,2000]{0,1:T(8,128)(2,1)}) %all-gather.4.cloned.1.call-update) | async-done | bytes 4096016 | tf_op jit(solution)/shard_map/all_gather | solution.py:177
  86.7 5.1 %fusion.4 = f32[512,1024]{1,0:T(8,128)S(1)} fusion(bf16[1024,2000]{0,1:T(8,128)(2,1)} %all-gather.4.cloned.1.call-done, bf16[384,2000]{0,1:T(8,128)(2,1)} %param.4, bf16[128,2000]{0,1:T(8,128)(2,1)} %param.5), kind=kOutput, calls=%fused_computation.4 | convolution fusion | flops 2101248000 | bytes 8241152 | tf_op jit(solution)/shard_map/dot_general | solution.py:175
  91.8 0.9 slice.16
  92.7 0.0 reduce-scatter.5.cloned.1.call-update
  92.7 0.0 reduce-scatter.7.cloned.1.call-start
  92.8 119.2 %all-gather.6.cloned.1.call-done = f32[1024,2048]{1,0:T(8,128)} async-done(((f32[128,2048]{1,0:T(8,128)}), f32[1024,2048]{1,0:T(8,128)}) %all-gather.6.cloned.1.call-update) | async-done | bytes 8388624 | tf_op jit(solution)/shard_map/all_gather | solution.py:183
  211.9 0.0 copy-done.2
  211.9 16.6 %fusion = f32[512,1024]{1,0:T(8,128)S(1)} fusion(f32[1024,2048]{1,0:T(8,128)} %all-gather.6.cloned.1.call-done, f32[384,2048]{1,0:T(8,128)} %param.6, f32[128,2048]{1,0:T(8,128)S(1)} %copy-done.2), kind=kOutput, calls=%fused_computation | convolution fusion | flops 12885950464 | bytes 14680064 | tf_op jit(solution)/shard_map/dot_general | solution.py:181
  228.6 0.0 copy-start.1
  228.6 1.3 copy-done.1
  229.9 0.8 slice.17
  230.8 0.0 reduce-scatter.7.cloned.1.call-update
  230.8 0.0 reduce-scatter.9.cloned.1.call-start
  230.8 1.3 slice.18
  232.1 0.0 reduce-scatter.9.cloned.1.call-update
  232.1 0.0 reduce-scatter.11.cloned.1.call-start
  232.2 2.8 slice.19
  235.0 0.0 reduce-scatter.11.cloned.1.call-update
  235.0 0.0 all-gather.8.cloned.1.call-start
  235.1 0.0 reduce-scatter.5.cloned.1.call-done
  235.1 24.0 %reduce-scatter.7.cloned.1.call-done = f32[128,256]{1,0:T(8,128)} async-done(((f32[128,1024]{1,0:T(8,128)}), f32[128,256]{1,0:T(8,128)}) %reduce-scatter.7.cloned.1.call-update) | async-done | bytes 131088 | tf_op jit(solution)/shard_map/reduce_scatter | solution.py:200
  259.1 1.1 add_subtract_fusion
  260.1 7.4 %all_gather.14 = f32[128,1024]{1,0:T(8,128)} all-gather(f32[128,256]{1,0:T(8,128)S(1)} %add_subtract_fusion), channel_id=1, replica_groups=mesh['grp'=4,'dev'=8] {'grp'}, dimensions={1}, use_global_device_ids=true | all-gather | bytes 655360 | tf_op jit(solution)/shard_map/all_gather | solution.py:203
  267.5 0.0 all-gather.8.cloned.1.call-update
  267.6 22.1 %reduce-scatter.9.cloned.1.call-done = f32[96,1024]{1,0:T(8,128)} async-done(((f32[384,1024]{1,0:T(8,128)}), f32[96,1024]{1,0:T(8,128)}) %reduce-scatter.9.cloned.1.call-update) | async-done | bytes 393232 | tf_op jit(solution)/shard_map/reduce_scatter | solution.py:189
  289.6 30.8 %reduce-scatter.11.cloned.1.call-done = f32[96,1024]{1,0:T(8,128)} async-done(((f32[384,1024]{1,0:T(8,128)}), f32[96,1024]{1,0:T(8,128)}) %reduce-scatter.11.cloned.1.call-update) | async-done | bytes 393232 | tf_op jit(solution)/shard_map/reduce_scatter | solution.py:190
  320.4 1.2 multiply_subtract_fusion.below_ref
  321.6 74.4 %all-gather.8.cloned.1.call-done.schur_ref = f32[1024,1024]{1,0:T(8,128)} async-done(((f32[128,1024]{1,0:T(8,128)}), f32[1024,1024]{1,0:T(8,128)}) %all-gather.8.cloned.1.call-update) | async-done | bytes 4194320 | tf_op jit(solution)/shard_map/all_gather | solution.py:204
  396.0 0.0 copy-start
  396.0 2.2 copy-done
  398.2 49.5 %cholesky_panel.1 = (f32[128,1024]{1,0:T(8,128)}, f32[96,1024]{1,0:T(8,128)}) custom-call(s32[1]{0:T(128)} %bitcast.place_ref, f32[1024,1024]{1,0:T(8,128)S(1)} %copy-done, f32[96,1024]{1,0:T(8,128)S(1)} %multiply_subtract_fusion.below_ref), custom_call_target="tpu_custom_call" | custom-call | tf_op jit(solution)/shard_map/cholesky_panel/pallas_call | solution.py:137
  (2 shorter events, 0.0 us)
Async XLA Ops:
  7.2 79.5 %all-gather.4.cloned.1.call-start = ((), (), s32[]{:S(2)}) async-start(), calls=%async_computation.4 | async-start | bytes 4608000 | tf_op jit(solution)/shard_map/all_gather | solution.py:177
  7.9 204.0 %all-gather.6.cloned.1.call-start = ((), (), s32[]{:S(2)}) async-start(), calls=%async_computation.6 | async-start | bytes 9437184 | tf_op jit(solution)/shard_map/all_gather | solution.py:183
  8.6 203.3 %copy-start.2 = (f32[128,2048]{1,0:T(8,128)S(1)}, f32[128,2048]{1,0:T(8,128)}, u32[]{:S(2)}) copy-start(f32[128,2048]{1,0:T(8,128)} %param.7) | copy-start | bytes 3145732
  8.7 226.4 %reduce-scatter.5.cloned.1.call-start = ((), (), s32[]{:S(2)}) async-start(), calls=%async_computation.5 | async-start | bytes 655360 | tf_op jit(solution)/shard_map/reduce_scatter | solution.py:199
  92.7 166.4 %reduce-scatter.7.cloned.1.call-start = ((), (), s32[]{:S(2)}) async-start(), calls=%async_computation.7 | async-start | bytes 655360 | tf_op jit(solution)/shard_map/reduce_scatter | solution.py:200
  228.6 1.3 copy-start.1
  230.8 58.9 %reduce-scatter.9.cloned.1.call-start = ((), (), s32[]{:S(2)}) async-start(), calls=%async_computation.9 | async-start | bytes 1966080 | tf_op jit(solution)/shard_map/reduce_scatter | solution.py:189
  232.1 88.3 %reduce-scatter.11.cloned.1.call-start = ((), (), s32[]{:S(2)}) async-start(), calls=%async_computation.10 | async-start | bytes 1966080 | tf_op jit(solution)/shard_map/reduce_scatter | solution.py:190
  235.0 161.0 %all-gather.8.cloned.1.call-start = ((), (), s32[]{:S(2)}) async-start(), calls=%async_computation.8 | async-start | bytes 4718592 | tf_op jit(solution)/shard_map/all_gather | solution.py:204
  396.0 2.2 copy-start
Sparse Core Ops, SparseCore 0:
  10.0 76.5 all-gather.3
  88.8 123.1 all-gather.5
  214.4 19.8 reduce-scatter.4
  237.4 21.6 reduce-scatter.6
  261.5 28.1 reduce-scatter.8
  292.2 28.1 reduce-scatter.10
  322.5 73.3 all-gather.7
